TPU v7x, 256 devices: a whole 4x4x8 slice. The times are simulated.
256 devices in a mesh: cpx: 16 (over y, z_lo, core), cpy: 16 (over x, z_hi).
Axes of the slice: x: 4, y: 4, z: 8 (z_hi: 4, z_lo: 2; z = z_hi * 2 + z_lo), core: 2. Of those that a mesh axis runs over, the one named last changes fastest.
Arguments:
- queries: bfloat16 [49152, 1024], P(('cpx', 'cpy')), may hold values from -6 to 6
- grad_out: bfloat16 [49152, 1024], P(('cpx', 'cpy')), may hold values from -60 to 60
- attn_out: bfloat16 [49152, 1024], P(('cpx', 'cpy')), may hold values from -6 to 6
- saved_lse: float32 [8, 49152], P(None, ('cpx', 'cpy')), may hold values from 6 to 8
- key_rows: bfloat16 [196608, 128], P(('cpx', 'cpy')), may hold values from -6 to 6
- value_rows: bfloat16 [196608, 128], P(('cpx', 'cpy')), may hold values from -6 to 6
- doc_lengths: int32 [64], replicated, may hold values from 1 to 6144, 196608 in all
- read_steps: int32 [256, 4], replicated, may hold values from -1 to 255, as said below
Outputs:
- grad_queries: float32 [49152, 1024], P(('cpx', 'cpy'))
- grad_keys: float32 [196608, 128], P(('cpx', 'cpy'))
- grad_values: float32 [196608, 128], P(('cpx', 'cpy'))
Inputs may be any that keep to these rules, and one draw needn't show every extreme that they name: `read_steps`: entry (d, t) is d - t if device d reads the key block of device d - t and -1 if not; entry (d, 0) is d; entries with d - t < 0 are -1.
All inputs are finite; a program needn't handle non-finite values.
Results may differ from a plain program's by a relative error of at most 0.0044.
Values may be sent and summed in bfloat16 or wider, within the bound.
No kernel may reach another device: no remote copies, remote signals or barrier semaphores. Data moves between devices by JAX's collectives and lax.ppermute only.
A program may use at most 64 MiB of HBM per device.

v0:
```python
import functools

import jax
import jax.numpy as jnp
from jax import lax
from jax.experimental import pallas as pl
from jax.experimental.pallas import tpu as pltpu
from jax.sharding import PartitionSpec as P

AXES = ("cpx", "cpy")
HEAD_DIM = 128
SCALE = HEAD_DIM**-0.5
LOG2E = 1.4426950408889634
KEY_TILE = 128
ROW_TILE = 512
LAST_BY_LAST = (((1,), (1,)), ((), ()))
FIRST_BY_FIRST = (((0,), (0,)), ((), ()))
F32, BF16, I32 = jnp.float32, jnp.bfloat16, jnp.int32


def passed_along(value, steps):
    count = lax.axis_size(AXES)
    return lax.ppermute(value, AXES, [(d, (d + steps) % count) for d in range(count)])


def make_weights(distance, k_ref, v_ref, q_ref, g_ref, stats_ref, w_ref, s_ref):
    block, flat = w_ref.shape
    rows = flat // 8

    for j in range(flat // ROW_TILE):
        cs = slice(j * ROW_TILE, (j + 1) * ROW_TILE)
        q, g = q_ref[cs, :], g_ref[cs, :]
        lse, delta = stats_ref[0:1, cs], stats_ref[1:2, cs]
        first_key = stats_ref[2:3, cs] + float(distance * block)
        for i in range(block // KEY_TILE):
            ks = slice(i * KEY_TILE, (i + 1) * KEY_TILE)
            scores = lax.dot_general(k_ref[ks, :], q, LAST_BY_LAST, preferred_element_type=F32)
            grad_w = lax.dot_general(v_ref[ks, :], g, LAST_BY_LAST, preferred_element_type=F32)
            key = (lax.broadcasted_iota(I32, (KEY_TILE, ROW_TILE), 0) + i * KEY_TILE).astype(F32)
            allowed = key >= first_key
            if distance == 0 and (i + 1) * KEY_TILE > block - rows:
                allowed = allowed & (key <= stats_ref[3:4, cs])
            weights = jnp.where(allowed, jnp.exp2(scores * (SCALE * LOG2E) - lse), 0.0)
            w_ref[ks, cs] = weights.astype(BF16)
            s_ref[ks, cs] = (weights * (grad_w - delta)).astype(BF16)


def key_value_grads(q_ref, g_ref, w_ref, s_ref, dk_ref, dv_ref):
    dk = jnp.dot(s_ref[...], q_ref[...], preferred_element_type=F32) * SCALE
    dk_ref[...] = dk.astype(dk_ref.dtype)
    dv_ref[...] = jnp.dot(w_ref[...], g_ref[...], preferred_element_type=F32).astype(dv_ref.dtype)


def query_grads(k_ref, s_ref):
    return lax.dot_general(k_ref[...], s_ref[...], FIRST_BY_FIRST, preferred_element_type=F32) * SCALE


def prepare_kernel(
    lens_hbm, steps_hbm, q_hbm, g_hbm, o_hbm, lse_hbm,
    q_ref, g_ref, stats_ref, flags_ref,
    o_ref, lse_ref, lens_ref, steps_ref, head_sems, sems, *, block,
):
    rows = q_hbm.shape[0]
    flat, head_dim = q_ref.shape
    heads = flat // rows
    device = lax.axis_index(AXES)
    small = [
        pltpu.make_async_copy(source, target, sems.at[i])
        for i, (source, target) in enumerate(
            [(lens_hbm, lens_ref), (steps_hbm, steps_ref), (lse_hbm, lse_ref)]
        )
    ]
    g_copies, o_copies, q_copies = (
        [
            pltpu.make_async_copy(
                source.at[:, h * head_dim : (h + 1) * head_dim],
                target.at[h * rows : (h + 1) * rows, :],
                head_sems.at[i, h],
            )
            for h in range(heads)
        ]
        for i, (source, target) in enumerate([(g_hbm, g_ref), (o_hbm, o_ref), (q_hbm, q_ref)])
    )
    for copy in small + g_copies + o_copies + q_copies:
        copy.start()
    for copy in small:
        copy.wait()
    for h in range(heads):
        stats_ref[0:1, h * rows : (h + 1) * rows] = lse_ref[h : h + 1, :] * LOG2E
    column = lax.broadcasted_iota(I32, (1, flat), 1)
    head = jnp.zeros((1, flat), I32)
    for h in range(1, heads):
        head = head + (column >= h * rows).astype(I32)
    local = column - head * rows + (block - rows)
    base = device * block
    query_pos = local + base

    def one_end(i, carry):
        end, starts, first = carry
        end = end + lens_ref[i]
        starts = jnp.where(query_pos >= end, end, starts)
        first = jnp.where(base + (block - rows) >= end, end, first)
        return end, starts, first

    zero = jnp.int32(0)
    _, starts, first = lax.fori_loop(
        0, lens_ref.shape[0], one_end, (zero, jnp.zeros((1, flat), I32), zero)
    )
    stats_ref[2:3, :] = (starts - base).astype(F32)
    stats_ref[3:4, :] = local.astype(F32)
    for t in range(steps_ref.shape[0]):
        owner = device - t
        active = (owner >= 0) & (steps_ref[t, device] == owner) & (first < (owner + 1) * block)
        flags_ref[t] = active.astype(I32)
    for copy in g_copies + o_copies:
        copy.wait()
    for c in range(flat // 128):
        cs = slice(c * 128, (c + 1) * 128)
        product = g_ref[cs, :].astype(F32) * o_ref[cs, :].astype(F32)
        stats_ref[1:2, cs] = jnp.sum(product.T, axis=0, keepdims=True)
    for copy in q_copies:
        copy.wait()


def block_kernel(
    distance, flags_ref, stats_ref, q_ref, g_ref, k_ref, v_ref, dk_ref, dv_ref, s_ref, w_ref
):
    @pl.when(flags_ref[distance] == 1)
    def _():
        make_weights(distance, k_ref, v_ref, q_ref, g_ref, stats_ref, w_ref, s_ref)
        key_value_grads(q_ref, g_ref, w_ref, s_ref, dk_ref, dv_ref)

    @pl.when(flags_ref[distance] == 0)
    def _():
        dk_ref[...] = jnp.zeros_like(dk_ref)
        dv_ref[...] = jnp.zeros_like(dv_ref)


def queries_kernel(flags_ref, *refs):
    count = (len(refs) - 2) // 2
    k_refs, s_refs, (out_ref, dq_ref) = refs[:count], refs[count : 2 * count], refs[2 * count :]
    rows, width = out_ref.shape
    head_dim = k_refs[0].shape[1]
    dq_ref[...] = jnp.zeros_like(dq_ref)
    for t in range(count):

        @pl.when(flags_ref[t] == 1)
        def _(t=t):
            dq_ref[...] += query_grads(k_refs[t], s_refs[t])

    by_row = dq_ref[...].T
    for h in range(width // head_dim):
        out_ref[:, h * head_dim : (h + 1) * head_dim] = by_row[h * rows : (h + 1) * rows, :]


def call(kernel, name, outs, scratch, args, places=None, smem_outs=(), flops=0, limit=40 << 20):
    vmem, smem = pl.BlockSpec(memory_space=pltpu.VMEM), pl.BlockSpec(memory_space=pltpu.SMEM)
    if places is None:
        places = [smem] + [vmem] * (len(args) - 1)
    return pl.pallas_call(
        kernel,
        name=name,
        out_shape=[jax.ShapeDtypeStruct(s, d) for s, d in outs],
        in_specs=places,
        out_specs=[smem if i in smem_outs else vmem for i in range(len(outs))],
        scratch_shapes=scratch,
        cost_estimate=pl.CostEstimate(flops=flops, bytes_accessed=0, transcendentals=0),
        compiler_params=pltpu.CompilerParams(vmem_limit_bytes=limit),
    )(*args)


def local(queries, grad_out, attn_out, saved_lse, key_rows, value_rows, doc_lengths, read_steps):
    rows, width = queries.shape
    block, head_dim = key_rows.shape
    heads = width // head_dim
    flat = rows * heads
    half = ((block, head_dim), BF16)
    full = ((block, head_dim), F32)
    scores = ((block, flat), BF16)
    flat_rows = ((flat, head_dim), BF16)
    total = ((head_dim, flat), F32)
    given = (doc_lengths, read_steps.T, queries, grad_out, attn_out, saved_lse)

    k1 = passed_along(key_rows, 1)
    v3 = passed_along(value_rows, 3)
    q, g, stats, flags = call(
        functools.partial(prepare_kernel, block=block), "prepare",
        [flat_rows, flat_rows, ((8, flat), F32), ((8,), I32)],
        [
            pltpu.VMEM(*flat_rows), pltpu.VMEM((heads, rows), F32),
            pltpu.SMEM(given[0].shape, I32), pltpu.SMEM(given[1].shape, I32),
            pltpu.SemaphoreType.DMA((3, heads)), pltpu.SemaphoreType.DMA((3,)),
        ],
        given, [pl.BlockSpec(memory_space=pltpu.HBM)] * 6, smem_outs=(3,), flops=20_000_000_000, limit=211 << 18,
    )

    def grads(distance, k, v, outs):
        return call(
            functools.partial(block_kernel, distance), f"block_{distance}",
            [*outs, scores], [pltpu.VMEM(*scores)], (flags, stats, q, g, k, v),
        )

    key_late, value_late, flags = lax.optimization_barrier((key_rows, value_rows, flags))
    v1 = passed_along(value_late, 1)
    k3 = passed_along(key_late, 3)
    dk0, dv0, s0 = grads(0, key_rows, value_rows, [full, full])
    k1, v3, s0 = lax.optimization_barrier((k1, v3, s0))
    k2 = passed_along(k1, 1)
    v2 = passed_along(v3, -1)
    v1, s0 = lax.optimization_barrier((v1, s0))
    dk1, dv1, s1 = grads(1, k1, v1, [full, half])
    dv1r = passed_along(dv1, -1)
    k2, v2, k3, s1 = lax.optimization_barrier((k2, v2, k3, s1))
    dk2, dv2, s2 = grads(2, k2, v2, [half, half])
    dk2r = passed_along(dk2, -1)
    dv2r = passed_along(dv2, 1)
    k3, s2, dv1r = lax.optimization_barrier((k3, s2, dv1r))
    dk3, dv3, s3 = grads(3, k3, v3, [half, full])
    dk3r = passed_along(dk3, -3)
    dv2r, dk2r, flags = lax.optimization_barrier((dv2r, dk2r, flags))
    dv3 = (dv3 + dv2r.astype(F32)).astype(BF16)
    dk2r, dv3 = lax.optimization_barrier((dk2r, dv3))
    dv3r = passed_along(dv3, -3)
    dk1r = passed_along((dk1 + dk2r.astype(F32)).astype(BF16), -1)
    (grad_queries,) = call(
        queries_kernel, "queries",
        [((rows, width), F32)], [pltpu.VMEM(*total)],
        (flags, key_rows, k1, k2, k3, s0, s1, s2, s3),
    )
    grad_keys = dk0 + dk3r.astype(F32) + dk1r.astype(F32)
    grad_values = dv0 + dv1r.astype(F32) + dv3r.astype(F32)
    return grad_queries, grad_keys, grad_values


def solution(mesh):
    return jax.shard_map(
        local,
        mesh=mesh,
        in_specs=(
            P(AXES, None),
            P(AXES, None),
            P(AXES, None),
            P(None, AXES),
            P(AXES, None),
            P(AXES, None),
            P(),
            P(),
        ),
        out_specs=(P(AXES, None), P(AXES, None), P(AXES, None)),
        check_vma=False,
    )
```

profile of v0, /device:TPU:46, one launch (start us, length us, event | category | flops | bytes accessed | tf_op | source)
XLA Modules:
  0.0 73.9 jit_solution(376444747071865651)
XLA Ops:
  0.6 5.5 %collective-permute-start.1 = (bf16[768,128]{1,0:T(8,128)(2,1)}, bf16[768,128]{1,0:T(8,128)(2,1)S(1)}, u32[]{:S(2)}, u32[]{:S(2)}) collective-permute-start(bf16[768,128]{1,0:T(8,128)(2,1)} %v_ref.1), channel_id=1, source_target_pairs={{0,3},{1,4},{2,5},{3,6},{4,7},{5,8},{6,9},{7,10},{8,11},{9,12},{10... | collective-permute-start | bytes 589832 | tf_op jit(solution)/shard_map/ppermute | solution.py:23
  6.1 0.0 collective-permute-start
  6.1 0.0 copy-start.2
  6.1 0.7 copy-done.2
  6.8 0.0 copy-start.3
  6.8 0.7 copy-done.3
  7.5 0.0 copy-start.4
  7.5 0.7 copy-done.4
  8.2 0.0 copy-start
  8.2 0.0 copy-start.1
  8.2 2.4 %prepare.1 = (bf16[1536,128]{1,0:T(8,128)(2,1)S(1)}, bf16[1536,128]{1,0:T(8,128)(2,1)S(1)}, f32[8,1536]{1,0:T(8,128)S(1)}, s32[8]{0:T(128)S(1)}) custom-call(s32[64]{0:T(128)S(1)} %copy-done.4, s32[4,256]{1,0:T(4,128)S(1)} %bitcast.1, bf16[192,1024]{1,0:T(8,128)(2,1)} %q_hbm.1, bf16[192,1024]{1,0:T(8,128)(2,1)} %g_hbm.1, bf16[192,1024]{1,0:T(8,128)(2,1)} %o_hbm.1, ...), custom_call_target="tpu_custom_call" | custom-call | flops 20000000000 | tf_op jit(solution)/shard_map/prepare/pallas_call | solution.py:160
  10.5 0.0 copy-done
  10.5 3.3 %collective-permute-start.4 = (bf16[768,128]{1,0:T(8,128)(2,1)S(1)}, bf16[768,128]{1,0:T(8,128)(2,1)S(1)}, u32[]{:S(2)}, u32[]{:S(2)}) collective-permute-start(bf16[768,128]{1,0:T(8,128)(2,1)S(1)} %copy-done), channel_id=1, source_target_pairs={{0,3},{1,4},{2,5},{3,6},{4,7},{5,8},{6,9},{7,10},{8,11},{9,12},{10... | collective-permute-start | bytes 589832 | tf_op jit(solution)/shard_map/ppermute | solution.py:23
  13.8 0.0 copy-done.1
  13.8 0.0 collective-permute-start.5
  13.8 3.5 %block_0.1 = (f32[768,128]{1,0:T(8,128)S(1)}, f32[768,128]{1,0:T(8,128)S(1)}, bf16[768,1536]{1,0:T(8,128)(2,1)S(1)}) custom-call(s32[8]{0:T(128)S(1)} %get-tuple-element.56.flags_ref, f32[8,1536]{1,0:T(8,128)S(1)} %get-tuple-element.41.stats_ref, bf16[1536,128]{1,0:T(8,128)(2,1)S(1)} %get-tuple-element.42.q_ref, ...), custom_call_target="tpu_custom_call" | custom-call | tf_op jit(solution)/shard_map/block_0/pallas_call | solution.py:160
  17.4 0.0 collective-permute-done.1.v_ref
  17.4 3.3 %collective-permute-done.k_ref.refs_1_ = bf16[768,128]{1,0:T(8,128)(2,1)S(1)} collective-permute-done((bf16[768,128]{1,0:T(8,128)(2,1)}, bf16[768,128]{1,0:T(8,128)(2,1)S(1)}, u32[]{:S(2)}, u32[]{:S(2)}) %collective-permute-start) | collective-permute-done | bytes 196640 | tf_op jit(solution)/shard_map/ppermute | solution.py:23
  20.7 1.8 %collective-permute-start.3 = (bf16[768,128]{1,0:T(8,128)(2,1)S(1)}, bf16[768,128]{1,0:T(8,128)(2,1)S(1)}, u32[]{:S(2)}, u32[]{:S(2)}) collective-permute-start(bf16[768,128]{1,0:T(8,128)(2,1)S(1)} %collective-permute-done.1.v_ref), channel_id=1, source_target_pairs={{0,255},{1,0},{2,1},{3,2},{4,3},{5,4},{6,5},{7,6},{8,7},{9,8},{10,... | collective-permute-start | bytes 589832 | tf_op jit(solution)/shard_map/ppermute | solution.py:23
  22.5 1.1 %collective-permute-start.2 = (bf16[768,128]{1,0:T(8,128)(2,1)S(1)}, bf16[768,128]{1,0:T(8,128)(2,1)S(1)}, u32[]{:S(2)}, u32[]{:S(2)}) collective-permute-start(bf16[768,128]{1,0:T(8,128)(2,1)S(1)} %collective-permute-done.k_ref.refs_1_), channel_id=1, source_target_pairs={{0,1},{1,2},{2,3},{3,4},{4,5},{5,6},{6,7},{7,8},{8,9},{9,10},{10,1... | collective-permute-start | bytes 589832 | tf_op jit(solution)/shard_map/ppermute | solution.py:23
  23.6 4.2 %collective-permute-done.5.v_ref = bf16[768,128]{1,0:T(8,128)(2,1)S(1)} collective-permute-done((bf16[768,128]{1,0:T(8,128)(2,1)S(1)}, bf16[768,128]{1,0:T(8,128)(2,1)S(1)}, u32[]{:S(2)}, u32[]{:S(2)}) %collective-permute-start.5) | collective-permute-done | bytes 196640 | tf_op jit(solution)/shard_map/ppermute | solution.py:23
  27.8 3.3 %block_1.1 = (f32[768,128]{1,0:T(8,128)S(1)}, bf16[768,128]{1,0:T(8,128)(2,1)S(1)}, bf16[768,1536]{1,0:T(8,128)(2,1)S(1)}) custom-call(s32[8]{0:T(128)S(1)} %get-tuple-element.56.flags_ref, f32[8,1536]{1,0:T(8,128)S(1)} %get-tuple-element.41.stats_ref, bf16[1536,128]{1,0:T(8,128)(2,1)S(1)} %get-tuple-element.42.q_ref, ...), custom_call_target="tpu_custom_call" | custom-call | tf_op jit(solution)/shard_map/block_1/pallas_call | solution.py:160
  31.1 0.1 collective-permute-start.8
  31.2 0.0 collective-permute-done.4.k_ref.refs_3_
  31.2 1.2 %collective-permute-done.3.v_ref = bf16[768,128]{1,0:T(8,128)(2,1)S(1)} collective-permute-done((bf16[768,128]{1,0:T(8,128)(2,1)S(1)}, bf16[768,128]{1,0:T(8,128)(2,1)S(1)}, u32[]{:S(2)}, u32[]{:S(2)}) %collective-permute-start.3) | collective-permute-done | bytes 196640 | tf_op jit(solution)/shard_map/ppermute | solution.py:23
  32.5 5.0 %collective-permute-done.2.k_ref.refs_2_ = bf16[768,128]{1,0:T(8,128)(2,1)S(1)} collective-permute-done((bf16[768,128]{1,0:T(8,128)(2,1)S(1)}, bf16[768,128]{1,0:T(8,128)(2,1)S(1)}, u32[]{:S(2)}, u32[]{:S(2)}) %collective-permute-start.2) | collective-permute-done | bytes 196640 | tf_op jit(solution)/shard_map/ppermute | solution.py:23
  37.5 3.5 %block_2.1 = (bf16[768,128]{1,0:T(8,128)(2,1)S(1)}, bf16[768,128]{1,0:T(8,128)(2,1)S(1)}, bf16[768,1536]{1,0:T(8,128)(2,1)S(1)}) custom-call(s32[8]{0:T(128)S(1)} %get-tuple-element.56.flags_ref, f32[8,1536]{1,0:T(8,128)S(1)} %get-tuple-element.41.stats_ref, bf16[1536,128]{1,0:T(8,128)(2,1)S(1)} %get-tuple-element.42.q_ref, ...), custom_call_target="tpu_custom_call" | custom-call | tf_op jit(solution)/shard_map/block_2/pallas_call | solution.py:160
  41.0 0.1 collective-permute-start.6
  41.1 5.0 %collective-permute-start.7 = (bf16[768,128]{1,0:T(8,128)(2,1)S(1)}, bf16[768,128]{1,0:T(8,128)(2,1)S(1)}, u32[]{:S(2)}, u32[]{:S(2)}) collective-permute-start(bf16[768,128]{1,0:T(8,128)(2,1)S(1)} %get-tuple-element.55), channel_id=1, source_target_pairs={{0,255},{1,0},{2,1},{3,2},{4,3},{5,4},{6,5},{7,6},{8,7},{9,8},{10,... | collective-permute-start | bytes 589832 | tf_op jit(solution)/shard_map/ppermute | solution.py:23
  46.1 0.0 collective-permute-done.8
  46.1 3.3 %block_3.1 = (bf16[768,128]{1,0:T(8,128)(2,1)S(1)}, f32[768,128]{1,0:T(8,128)S(1)}, bf16[768,1536]{1,0:T(8,128)(2,1)S(1)}) custom-call(s32[8]{0:T(128)S(1)} %get-tuple-element.56.flags_ref, f32[8,1536]{1,0:T(8,128)S(1)} %get-tuple-element.41.stats_ref, bf16[1536,128]{1,0:T(8,128)(2,1)S(1)} %get-tuple-element.42.q_ref, ...), custom_call_target="tpu_custom_call" | custom-call | tf_op jit(solution)/shard_map/block_3/pallas_call | solution.py:160
  49.4 0.1 collective-permute-start.9
  49.5 8.5 %collective-permute-done.6 = bf16[768,128]{1,0:T(8,128)(2,1)S(1)} collective-permute-done((bf16[768,128]{1,0:T(8,128)(2,1)S(1)}, bf16[768,128]{1,0:T(8,128)(2,1)S(1)}, u32[]{:S(2)}, u32[]{:S(2)}) %collective-permute-start.6) | collective-permute-done | bytes 196640 | tf_op jit(solution)/shard_map/ppermute | solution.py:23
  58.0 0.0 collective-permute-done.7
  58.0 0.1 add_convert_fusion.1
  58.1 0.1 collective-permute-start.11
  58.2 0.1 add_convert_fusion
  58.2 0.4 collective-permute-start.10
  58.6 3.8 %queries.1 = f32[192,1024]{1,0:T(8,128)} custom-call(s32[8]{0:T(128)S(1)} %get-tuple-element.56.flags_ref, bf16[768,128]{1,0:T(8,128)(2,1)S(1)} %copy-done, bf16[768,128]{1,0:T(8,128)(2,1)S(1)} %collective-permute-done.k_ref.refs_1_, bf16[768,128]{1,0:T(8,128)(2,1)S(1)} %collective-permute-done.2.k_ref.refs_2_, ...), custom_call_target="tpu_custom_call" | custom-call | tf_op jit(solution)/shard_map/queries/pallas_call | solution.py:160
  62.4 9.9 %collective-permute-done.11 = bf16[768,128]{1,0:T(8,128)(2,1)S(1)} collective-permute-done((bf16[768,128]{1,0:T(8,128)(2,1)S(1)}, bf16[768,128]{1,0:T(8,128)(2,1)S(1)}, u32[]{:S(2)}, u32[]{:S(2)}) %collective-permute-start.11) | collective-permute-done | bytes 196640 | tf_op jit(solution)/shard_map/ppermute | solution.py:23
  72.3 0.8 %convert_add_fusion = f32[768,128]{1,0:T(8,128)} fusion(bf16[768,128]{1,0:T(8,128)(2,1)S(1)} %collective-permute-done.11, f32[768,128]{1,0:T(8,128)S(1)} %get-tuple-element.72, bf16[768,128]{1,0:T(8,128)(2,1)S(1)} %collective-permute-done.8), kind=kLoop, calls=%fused_computation | loop fusion | flops 393216 | bytes 1179648 | tf_op jit(solution)/shard_map/add | solution.py:231
  73.1 0.0 collective-permute-done.9
  73.1 0.0 collective-permute-done.10
  73.1 0.8 %convert_add_fusion.1 = f32[768,128]{1,0:T(8,128)} fusion(bf16[768,128]{1,0:T(8,128)(2,1)S(1)} %collective-permute-done.10, f32[768,128]{1,0:T(8,128)S(1)} %get-tuple-element.65, bf16[768,128]{1,0:T(8,128)(2,1)S(1)} %collective-permute-done.9), kind=kLoop, calls=%fused_computation.1 | loop fusion | flops 393216 | bytes 1179648 | tf_op jit(solution)/shard_map/add | solution.py:230
Async XLA Ops:
  0.6 16.7 %collective-permute-start.1 = (bf16[768,128]{1,0:T(8,128)(2,1)}, bf16[768,128]{1,0:T(8,128)(2,1)S(1)}, u32[]{:S(2)}, u32[]{:S(2)}) collective-permute-start(bf16[768,128]{1,0:T(8,128)(2,1)} %v_ref.1), channel_id=1, source_target_pairs={{0,3},{1,4},{2,5},{3,6},{4,7},{5,8},{6,9},{7,10},{8,11},{9,12},{10... | collective-permute-start | bytes 589832 | tf_op jit(solution)/shard_map/ppermute | solution.py:23
  6.1 14.6 %collective-permute-start = (bf16[768,128]{1,0:T(8,128)(2,1)}, bf16[768,128]{1,0:T(8,128)(2,1)S(1)}, u32[]{:S(2)}, u32[]{:S(2)}) collective-permute-start(bf16[768,128]{1,0:T(8,128)(2,1)} %refs_0_.1), channel_id=1, source_target_pairs={{0,1},{1,2},{2,3},{3,4},{4,5},{5,6},{6,7},{7,8},{8,9},{9,10},{10,1... | collective-permute-start | bytes 589832 | tf_op jit(solution)/shard_map/ppermute | solution.py:23
  6.1 0.7 copy-start.2
  6.8 0.7 copy-start.3
  7.5 0.7 copy-start.4
  8.2 2.4 %copy-start = (bf16[768,128]{1,0:T(8,128)(2,1)S(1)}, bf16[768,128]{1,0:T(8,128)(2,1)}, u32[]{:S(2)}) copy-start(bf16[768,128]{1,0:T(8,128)(2,1)} %refs_0_.1) | copy-start | bytes 589828
  8.2 5.7 %copy-start.1 = (bf16[768,128]{1,0:T(8,128)(2,1)S(1)}, bf16[768,128]{1,0:T(8,128)(2,1)}, u32[]{:S(2)}) copy-start(bf16[768,128]{1,0:T(8,128)(2,1)} %v_ref.1) | copy-start | bytes 589828
  10.5 20.7 %collective-permute-start.4 = (bf16[768,128]{1,0:T(8,128)(2,1)S(1)}, bf16[768,128]{1,0:T(8,128)(2,1)S(1)}, u32[]{:S(2)}, u32[]{:S(2)}) collective-permute-start(bf16[768,128]{1,0:T(8,128)(2,1)S(1)} %copy-done), channel_id=1, source_target_pairs={{0,3},{1,4},{2,5},{3,6},{4,7},{5,8},{6,9},{7,10},{8,11},{9,12},{10... | collective-permute-start | bytes 589832 | tf_op jit(solution)/shard_map/ppermute | solution.py:23
  13.8 14.0 %collective-permute-start.5 = (bf16[768,128]{1,0:T(8,128)(2,1)S(1)}, bf16[768,128]{1,0:T(8,128)(2,1)S(1)}, u32[]{:S(2)}, u32[]{:S(2)}) collective-permute-start(bf16[768,128]{1,0:T(8,128)(2,1)S(1)} %copy-done.1), channel_id=1, source_target_pairs={{0,1},{1,2},{2,3},{3,4},{4,5},{5,6},{6,7},{7,8},{8,9},{9,10},{10,1... | collective-permute-start | bytes 589832 | tf_op jit(solution)/shard_map/ppermute | solution.py:23
  20.7 11.8 %collective-permute-start.3 = (bf16[768,128]{1,0:T(8,128)(2,1)S(1)}, bf16[768,128]{1,0:T(8,128)(2,1)S(1)}, u32[]{:S(2)}, u32[]{:S(2)}) collective-permute-start(bf16[768,128]{1,0:T(8,128)(2,1)S(1)} %collective-permute-done.1.v_ref), channel_id=1, source_target_pairs={{0,255},{1,0},{2,1},{3,2},{4,3},{5,4},{6,5},{7,6},{8,7},{9,8},{10,... | collective-permute-start | bytes 589832 | tf_op jit(solution)/shard_map/ppermute | solution.py:23
  22.5 14.9 %collective-permute-start.2 = (bf16[768,128]{1,0:T(8,128)(2,1)S(1)}, bf16[768,128]{1,0:T(8,128)(2,1)S(1)}, u32[]{:S(2)}, u32[]{:S(2)}) collective-permute-start(bf16[768,128]{1,0:T(8,128)(2,1)S(1)} %collective-permute-done.k_ref.refs_1_), channel_id=1, source_target_pairs={{0,1},{1,2},{2,3},{3,4},{4,5},{5,6},{6,7},{7,8},{8,9},{9,10},{10,1... | collective-permute-start | bytes 589832 | tf_op jit(solution)/shard_map/ppermute | solution.py:23
  31.1 15.0 %collective-permute-start.8 = (bf16[768,128]{1,0:T(8,128)(2,1)S(1)}, bf16[768,128]{1,0:T(8,128)(2,1)S(1)}, u32[]{:S(2)}, u32[]{:S(2)}) collective-permute-start(bf16[768,128]{1,0:T(8,128)(2,1)S(1)} %get-tuple-element.59), channel_id=1, source_target_pairs={{0,255},{1,0},{2,1},{3,2},{4,3},{5,4},{6,5},{7,6},{8,7},{9,8},{10,... | collective-permute-start | bytes 589832 | tf_op jit(solution)/shard_map/ppermute | solution.py:23
  41.0 17.0 %collective-permute-start.6 = (bf16[768,128]{1,0:T(8,128)(2,1)S(1)}, bf16[768,128]{1,0:T(8,128)(2,1)S(1)}, u32[]{:S(2)}, u32[]{:S(2)}) collective-permute-start(bf16[768,128]{1,0:T(8,128)(2,1)S(1)} %get-tuple-element.54), channel_id=1, source_target_pairs={{0,1},{1,2},{2,3},{3,4},{4,5},{5,6},{6,7},{7,8},{8,9},{9,10},{10,1... | collective-permute-start | bytes 589832 | tf_op jit(solution)/shard_map/ppermute | solution.py:23
  41.1 16.9 %collective-permute-start.7 = (bf16[768,128]{1,0:T(8,128)(2,1)S(1)}, bf16[768,128]{1,0:T(8,128)(2,1)S(1)}, u32[]{:S(2)}, u32[]{:S(2)}) collective-permute-start(bf16[768,128]{1,0:T(8,128)(2,1)S(1)} %get-tuple-element.55), channel_id=1, source_target_pairs={{0,255},{1,0},{2,1},{3,2},{4,3},{5,4},{6,5},{7,6},{8,7},{9,8},{10,... | collective-permute-start | bytes 589832 | tf_op jit(solution)/shard_map/ppermute | solution.py:23
  49.4 23.7 %collective-permute-start.9 = (bf16[768,128]{1,0:T(8,128)(2,1)S(1)}, bf16[768,128]{1,0:T(8,128)(2,1)S(1)}, u32[]{:S(2)}, u32[]{:S(2)}) collective-permute-start(bf16[768,128]{1,0:T(8,128)(2,1)S(1)} %get-tuple-element.66), channel_id=1, source_target_pairs={{0,253},{1,254},{2,255},{3,0},{4,1},{5,2},{6,3},{7,4},{8,5},{9,6},... | collective-permute-start | bytes 589832 | tf_op jit(solution)/shard_map/ppermute | solution.py:23
  58.1 14.2 %collective-permute-start.11 = (bf16[768,128]{1,0:T(8,128)(2,1)S(1)}, bf16[768,128]{1,0:T(8,128)(2,1)S(1)}, u32[]{:S(2)}, u32[]{:S(2)}) collective-permute-start(bf16[768,128]{1,0:T(8,128)(2,1)S(1)} %add_convert_fusion.1), channel_id=1, source_target_pairs={{0,253},{1,254},{2,255},{3,0},{4,1},{5,2},{6,3},{7,4},{8,5},{9,6},... | collective-permute-start | bytes 589832 | tf_op jit(solution)/shard_map/ppermute | solution.py:23
  58.2 14.9 %collective-permute-start.10 = (bf16[768,128]{1,0:T(8,128)(2,1)S(1)}, bf16[768,128]{1,0:T(8,128)(2,1)S(1)}, u32[]{:S(2)}, u32[]{:S(2)}) collective-permute-start(bf16[768,128]{1,0:T(8,128)(2,1)S(1)} %add_convert_fusion), channel_id=1, source_target_pairs={{0,255},{1,0},{2,1},{3,2},{4,3},{5,4},{6,5},{7,6},{8,7},{9,8},{10,... | collective-permute-start | bytes 589832 | tf_op jit(solution)/shard_map/ppermute | solution.py:23
where the time goes:
time: 73.7 us; the launch traced here: 73.9 us
  waiting for transfers between devices  32.1 us (44%)
  Pallas kernels  19.8 us (27%)
  starting transfers between devices  17.5 us (24%)
  local copies, waits for them, and re-layouts  2.05 us (3%)
  other arithmetic  1.75 us (2%)
  between operations  0.74 us (1%)
    ppermute x12, waiting for transfers between devices, passed_along(): lax.ppermute(value, AXES, [(d, (d + steps) % count) for d in range(count)])  32.1 us
    pallas_call x6, Pallas kernels, call(): pl.pallas_call(kernel, name=name, out_shape=[jax.ShapeDtypeStruct(s, d) f...  19.8 us
    ppermute x12, starting transfers between devices, passed_along(): lax.ppermute(value, AXES, [(d, (d + steps) % count) for d in range(count)])  17.5 us
    unnamed x10, local copies, waits for them, and re-layouts  2.05 us
  transfers between devices with their start and end apart: 12, of which 6 were waited for; matrix products, arithmetic and copies ran while one was open for 1% of the time, Pallas kernels for 27%

commit v1 on v0

--- a/solution.py
+++ b/solution.py
@@ -55,38 +55,44 @@
     return lax.dot_general(k_ref[...], s_ref[...], FIRST_BY_FIRST, preferred_element_type=F32) * SCALE
 
 
-def prepare_kernel(
-    lens_hbm, steps_hbm, q_hbm, g_hbm, o_hbm, lse_hbm,
-    q_ref, g_ref, stats_ref, flags_ref,
-    o_ref, lse_ref, lens_ref, steps_ref, head_sems, sems, *, block,
-):
+def prepare_kernel(q_hbm, g_hbm, o_hbm, q_ref, g_ref, delta_ref, o_ref, sems):
     rows = q_hbm.shape[0]
     flat, head_dim = q_ref.shape
     heads = flat // rows
-    device = lax.axis_index(AXES)
-    small = [
-        pltpu.make_async_copy(source, target, sems.at[i])
-        for i, (source, target) in enumerate(
-            [(lens_hbm, lens_ref), (steps_hbm, steps_ref), (lse_hbm, lse_ref)]
-        )
-    ]
     g_copies, o_copies, q_copies = (
         [
             pltpu.make_async_copy(
                 source.at[:, h * head_dim : (h + 1) * head_dim],
                 target.at[h * rows : (h + 1) * rows, :],
-                head_sems.at[i, h],
+                sems.at[i, h],
             )
             for h in range(heads)
         ]
         for i, (source, target) in enumerate([(g_hbm, g_ref), (o_hbm, o_ref), (q_hbm, q_ref)])
     )
-    for copy in small + g_copies + o_copies + q_copies:
+    for copy in g_copies + o_copies + q_copies:
         copy.start()
-    for copy in small:
+    for copy in g_copies + o_copies:
         copy.wait()
+    for c in range(flat // 128):
+        cs = slice(c * 128, (c + 1) * 128)
+        product = g_ref[cs, :].astype(F32) * o_ref[cs, :].astype(F32)
+        delta_ref[0:1, cs] = jnp.sum(product.T, axis=0, keepdims=True)
+    for copy in q_copies:
+        copy.wait()
+
+
+def own_kernel(
+    lens_ref, steps_ref, lse_ref, delta_ref, q_ref, g_ref, k_ref, v_ref,
+    stats_ref, flags_ref, dk_ref, dv_ref, s_ref, w_ref,
+):
+    heads, rows = lse_ref.shape
+    flat = heads * rows
+    block = k_ref.shape[0]
+    device = lax.axis_index(AXES)
     for h in range(heads):
         stats_ref[0:1, h * rows : (h + 1) * rows] = lse_ref[h : h + 1, :] * LOG2E
+    stats_ref[1:2, :] = delta_ref[0:1, :]
     column = lax.broadcasted_iota(I32, (1, flat), 1)
     head = jnp.zeros((1, flat), I32)
     for h in range(1, heads):
@@ -112,14 +118,9 @@
         owner = device - t
         active = (owner >= 0) & (steps_ref[t, device] == owner) & (first < (owner + 1) * block)
         flags_ref[t] = active.astype(I32)
-    for copy in g_copies + o_copies:
-        copy.wait()
-    for c in range(flat // 128):
-        cs = slice(c * 128, (c + 1) * 128)
-        product = g_ref[cs, :].astype(F32) * o_ref[cs, :].astype(F32)
-        stats_ref[1:2, cs] = jnp.sum(product.T, axis=0, keepdims=True)
-    for copy in q_copies:
-        copy.wait()
+    block_kernel(
+        0, flags_ref, stats_ref, q_ref, g_ref, k_ref, v_ref, dk_ref, dv_ref, s_ref, w_ref
+    )
 
 
 def block_kernel(
@@ -179,19 +180,16 @@
     scores = ((block, flat), BF16)
     flat_rows = ((flat, head_dim), BF16)
     total = ((head_dim, flat), F32)
-    given = (doc_lengths, read_steps.T, queries, grad_out, attn_out, saved_lse)
-
     k1 = passed_along(key_rows, 1)
     v3 = passed_along(value_rows, 3)
-    q, g, stats, flags = call(
-        functools.partial(prepare_kernel, block=block), "prepare",
-        [flat_rows, flat_rows, ((8, flat), F32), ((8,), I32)],
-        [
-            pltpu.VMEM(*flat_rows), pltpu.VMEM((heads, rows), F32),
-            pltpu.SMEM(given[0].shape, I32), pltpu.SMEM(given[1].shape, I32),
-            pltpu.SemaphoreType.DMA((3, heads)), pltpu.SemaphoreType.DMA((3,)),
-        ],
-        given, [pl.BlockSpec(memory_space=pltpu.HBM)] * 6, smem_outs=(3,), flops=20_000_000_000, limit=211 << 18,
+    vmem, smem, hbm = (
+        pl.BlockSpec(memory_space=space) for space in (pltpu.VMEM, pltpu.SMEM, pltpu.HBM)
+    )
+    q, g, delta = call(
+        prepare_kernel, "prepare",
+        [flat_rows, flat_rows, ((8, flat), F32)],
+        [pltpu.VMEM(*flat_rows), pltpu.SemaphoreType.DMA((3, heads))],
+        (queries, grad_out, attn_out), [hbm] * 3, flops=20_000_000_000, limit=212 << 18,
     )
 
     def grads(distance, k, v, outs):
@@ -200,11 +198,17 @@
             [*outs, scores], [pltpu.VMEM(*scores)], (flags, stats, q, g, k, v),
         )
 
-    key_late, value_late, flags = lax.optimization_barrier((key_rows, value_rows, flags))
+    key_late, value_late, delta = lax.optimization_barrier((key_rows, value_rows, delta))
     v1 = passed_along(value_late, 1)
     k3 = passed_along(key_late, 3)
-    dk0, dv0, s0 = grads(0, key_rows, value_rows, [full, full])
-    k1, v3, s0 = lax.optimization_barrier((k1, v3, s0))
+    stats, flags, dk0, dv0, s0 = call(
+        own_kernel, "block_0",
+        [((8, flat), F32), ((8,), I32), full, full, scores], [pltpu.VMEM(*scores)],
+        (doc_lengths, read_steps.T, saved_lse, delta, q, g, key_rows, value_rows),
+        [smem] * 2 + [vmem] * 6, smem_outs=(1,),
+    )
+    k1, s0_a = lax.optimization_barrier((k1, s0))
+    v3, s0_b = lax.optimization_barrier((v3, s0))
     k2 = passed_along(k1, 1)
     v2 = passed_along(v3, -1)
     v1, s0 = lax.optimization_barrier((v1, s0))

time: 73.7 us -> 75.1 us (1.019)
  the two profiles are of different devices: /device:TPU:46 before, /device:TPU:7 now
where the time goes in v1:
time: 75.1 us; the launch traced here: 74.9 us
  waiting for transfers between devices  34.5 us (46%)
  starting transfers between devices  23.9 us (32%)
  Pallas kernels  13.9 us (19%)
  other arithmetic  1.72 us (2%)
  between operations  0.8 us (1%)
    ppermute x12, waiting for transfers between devices, passed_along(): lax.ppermute(value, AXES, [(d, (d + steps) % count) for d in range(count)])  34.5 us
    ppermute x12, starting transfers between devices, passed_along(): lax.ppermute(value, AXES, [(d, (d + steps) % count) for d in range(count)])  23.9 us
    pallas_call x6, Pallas kernels, call(): pl.pallas_call(kernel, name=name, out_shape=[jax.ShapeDtypeStruct(s, d) f...  13.9 us
  transfers between devices with their start and end apart: 12, of which 4 were waited for; matrix products, arithmetic and copies ran while one was open for 1% of the time, Pallas kernels for 19%

profile of v1, /device:TPU:7, one launch (start us, length us, event | category | flops | bytes accessed | tf_op | source)
XLA Modules:
  0.0 74.9 jit_solution(9373781621953345188)
XLA Ops:
  0.6 0.0 copy-start.1
  0.6 0.0 copy-start
  0.7 0.0 copy-start.3
  0.7 0.0 copy-start.4
  0.7 0.0 copy-start.2
  0.7 6.1 %collective-permute-start.2 = (bf16[768,128]{1,0:T(8,128)(2,1)}, bf16[768,128]{1,0:T(8,128)(2,1)S(1)}, u32[]{:S(2)}, u32[]{:S(2)}) collective-permute-start(bf16[768,128]{1,0:T(8,128)(2,1)} %v_ref.1), channel_id=1, source_target_pairs={{0,3},{1,4},{2,5},{3,6},{4,7},{5,8},{6,9},{7,10},{8,11},{9,12},{10... | collective-permute-start | bytes 589832 | tf_op jit(solution)/shard_map/ppermute | solution.py:23
  6.8 0.0 collective-permute-start
  6.8 1.6 %prepare.1 = (bf16[1536,128]{1,0:T(8,128)(2,1)S(1)}, bf16[1536,128]{1,0:T(8,128)(2,1)S(1)}, f32[8,1536]{1,0:T(8,128)S(1)}) custom-call(bf16[192,1024]{1,0:T(8,128)(2,1)} %q_hbm.1, bf16[192,1024]{1,0:T(8,128)(2,1)} %g_hbm.1, bf16[192,1024]{1,0:T(8,128)(2,1)} %o_hbm.1), custom_call_target="tpu_custom_call" | custom-call | flops 20000000000 | tf_op jit(solution)/shard_map/prepare/pallas_call | solution.py:161
  8.4 0.0 copy-done
  8.5 4.9 %collective-permute-start.4 = (bf16[768,128]{1,0:T(8,128)(2,1)S(1)}, bf16[768,128]{1,0:T(8,128)(2,1)S(1)}, u32[]{:S(2)}, u32[]{:S(2)}) collective-permute-start(bf16[768,128]{1,0:T(8,128)(2,1)S(1)} %copy-done), channel_id=1, source_target_pairs={{0,3},{1,4},{2,5},{3,6},{4,7},{5,8},{6,9},{7,10},{8,11},{9,12},{10... | collective-permute-start | bytes 589832 | tf_op jit(solution)/shard_map/ppermute | solution.py:23
  13.3 0.0 copy-done.1
  13.3 0.0 collective-permute-start.5
  13.3 0.0 copy-done.3
  13.3 0.0 copy-done.4
  13.3 0.0 copy-done.2
  13.3 4.8 %block_0.1 = (f32[8,1536]{1,0:T(8,128)S(1)}, s32[8]{0:T(128)S(1)}, f32[768,128]{1,0:T(8,128)S(1)}, f32[768,128]{1,0:T(8,128)S(1)}, bf16[768,1536]{1,0:T(8,128)(2,1)S(1)}) custom-call(s32[64]{0:T(128)S(1)} %copy-done.4, s32[4,256]{1,0:T(4,128)S(1)} %bitcast.1, f32[8,192]{1,0:T(8,128)S(1)} %copy-done.2, f32[8,1536]{1,0:T(8,128)S(1)} %get-tuple-element.40.delta_ref, ...), custom_call_target="tpu_custom_call" | custom-call | tf_op jit(solution)/shard_map/block_0/pallas_call | solution.py:161
  18.2 0.0 collective-permute-done.2.v_ref
  18.2 0.0 collective-permute-done.k_ref.refs_1_
  18.2 1.8 %collective-permute-start.1 = (bf16[768,128]{1,0:T(8,128)(2,1)S(1)}, bf16[768,128]{1,0:T(8,128)(2,1)S(1)}, u32[]{:S(2)}, u32[]{:S(2)}) collective-permute-start(bf16[768,128]{1,0:T(8,128)(2,1)S(1)} %collective-permute-done.k_ref.refs_1_), channel_id=1, source_target_pairs={{0,1},{1,2},{2,3},{3,4},{4,5},{5,6},{6,7},{7,8},{8,9},{9,10},{10,1... | collective-permute-start | bytes 589832 | tf_op jit(solution)/shard_map/ppermute | solution.py:23
  20.0 2.8 %collective-permute-start.3 = (bf16[768,128]{1,0:T(8,128)(2,1)S(1)}, bf16[768,128]{1,0:T(8,128)(2,1)S(1)}, u32[]{:S(2)}, u32[]{:S(2)}) collective-permute-start(bf16[768,128]{1,0:T(8,128)(2,1)S(1)} %collective-permute-done.2.v_ref), channel_id=1, source_target_pairs={{0,255},{1,0},{2,1},{3,2},{4,3},{5,4},{6,5},{7,6},{8,7},{9,8},{10,... | collective-permute-start | bytes 589832 | tf_op jit(solution)/shard_map/ppermute | solution.py:23
  22.8 4.1 %collective-permute-done.5.v_ref = bf16[768,128]{1,0:T(8,128)(2,1)S(1)} collective-permute-done((bf16[768,128]{1,0:T(8,128)(2,1)S(1)}, bf16[768,128]{1,0:T(8,128)(2,1)S(1)}, u32[]{:S(2)}, u32[]{:S(2)}) %collective-permute-start.5) | collective-permute-done | bytes 196640 | tf_op jit(solution)/shard_map/ppermute | solution.py:23
  26.9 3.3 %block_1.1 = (f32[768,128]{1,0:T(8,128)S(1)}, bf16[768,128]{1,0:T(8,128)(2,1)S(1)}, bf16[768,1536]{1,0:T(8,128)(2,1)S(1)}) custom-call(s32[8]{0:T(128)S(1)} %get-tuple-element.56.flags_ref, f32[8,1536]{1,0:T(8,128)S(1)} %get-tuple-element.44.stats_ref, bf16[1536,128]{1,0:T(8,128)(2,1)S(1)} %get-tuple-element.41.q_ref, ...), custom_call_target="tpu_custom_call" | custom-call | tf_op jit(solution)/shard_map/block_1/pallas_call | solution.py:161
  30.2 0.1 collective-permute-start.8
  30.3 0.0 collective-permute-done.4.k_ref.refs_3_
  30.3 7.3 %collective-permute-done.1.k_ref.refs_2_ = bf16[768,128]{1,0:T(8,128)(2,1)S(1)} collective-permute-done((bf16[768,128]{1,0:T(8,128)(2,1)S(1)}, bf16[768,128]{1,0:T(8,128)(2,1)S(1)}, u32[]{:S(2)}, u32[]{:S(2)}) %collective-permute-start.1) | collective-permute-done | bytes 196640 | tf_op jit(solution)/shard_map/ppermute | solution.py:23
  37.6 0.0 collective-permute-done.3.v_ref
  37.6 0.8 %block_2.1 = (bf16[768,128]{1,0:T(8,128)(2,1)S(1)}, bf16[768,128]{1,0:T(8,128)(2,1)S(1)}, bf16[768,1536]{1,0:T(8,128)(2,1)S(1)}) custom-call(s32[8]{0:T(128)S(1)} %get-tuple-element.56.flags_ref, f32[8,1536]{1,0:T(8,128)S(1)} %get-tuple-element.44.stats_ref, bf16[1536,128]{1,0:T(8,128)(2,1)S(1)} %get-tuple-element.41.q_ref, ...), custom_call_target="tpu_custom_call" | custom-call | tf_op jit(solution)/shard_map/block_2/pallas_call | solution.py:161
  38.4 0.1 collective-permute-start.6
  38.5 4.5 %collective-permute-start.7 = (bf16[768,128]{1,0:T(8,128)(2,1)S(1)}, bf16[768,128]{1,0:T(8,128)(2,1)S(1)}, u32[]{:S(2)}, u32[]{:S(2)}) collective-permute-start(bf16[768,128]{1,0:T(8,128)(2,1)S(1)} %get-tuple-element.55), channel_id=1, source_target_pairs={{0,255},{1,0},{2,1},{3,2},{4,3},{5,4},{6,5},{7,6},{8,7},{9,8},{10,... | collective-permute-start | bytes 589832 | tf_op jit(solution)/shard_map/ppermute | solution.py:23
  42.9 0.0 collective-permute-done.8
  42.9 0.6 block_3.1
  43.5 0.1 collective-permute-start.9
  43.6 8.8 %collective-permute-done.6 = bf16[768,128]{1,0:T(8,128)(2,1)S(1)} collective-permute-done((bf16[768,128]{1,0:T(8,128)(2,1)S(1)}, bf16[768,128]{1,0:T(8,128)(2,1)S(1)}, u32[]{:S(2)}, u32[]{:S(2)}) %collective-permute-start.6) | collective-permute-done | bytes 196640 | tf_op jit(solution)/shard_map/ppermute | solution.py:23
  52.5 0.0 collective-permute-done.7
  52.5 0.1 add_convert_fusion.1
  52.5 2.5 %collective-permute-start.11 = (bf16[768,128]{1,0:T(8,128)(2,1)S(1)}, bf16[768,128]{1,0:T(8,128)(2,1)S(1)}, u32[]{:S(2)}, u32[]{:S(2)}) collective-permute-start(bf16[768,128]{1,0:T(8,128)(2,1)S(1)} %add_convert_fusion.1), channel_id=1, source_target_pairs={{0,253},{1,254},{2,255},{3,0},{4,1},{5,2},{6,3},{7,4},{8,5},{9,6},... | collective-permute-start | bytes 589832 | tf_op jit(solution)/shard_map/ppermute | solution.py:23
  55.0 0.1 add_convert_fusion
  55.1 1.1 %collective-permute-start.10 = (bf16[768,128]{1,0:T(8,128)(2,1)S(1)}, bf16[768,128]{1,0:T(8,128)(2,1)S(1)}, u32[]{:S(2)}, u32[]{:S(2)}) collective-permute-start(bf16[768,128]{1,0:T(8,128)(2,1)S(1)} %add_convert_fusion), channel_id=1, source_target_pairs={{0,255},{1,0},{2,1},{3,2},{4,3},{5,4},{6,5},{7,6},{8,7},{9,8},{10,... | collective-permute-start | bytes 589832 | tf_op jit(solution)/shard_map/ppermute | solution.py:23
  56.2 2.8 %queries.1 = f32[192,1024]{1,0:T(8,128)} custom-call(s32[8]{0:T(128)S(1)} %get-tuple-element.56.flags_ref, bf16[768,128]{1,0:T(8,128)(2,1)S(1)} %copy-done, bf16[768,128]{1,0:T(8,128)(2,1)S(1)} %collective-permute-done.k_ref.refs_1_, bf16[768,128]{1,0:T(8,128)(2,1)S(1)} %collective-permute-done.1.k_ref.refs_2_, ...), custom_call_target="tpu_custom_call" | custom-call | tf_op jit(solution)/shard_map/queries/pallas_call | solution.py:161
  59.0 14.3 %collective-permute-done.11 = bf16[768,128]{1,0:T(8,128)(2,1)S(1)} collective-permute-done((bf16[768,128]{1,0:T(8,128)(2,1)S(1)}, bf16[768,128]{1,0:T(8,128)(2,1)S(1)}, u32[]{:S(2)}, u32[]{:S(2)}) %collective-permute-start.11) | collective-permute-done | bytes 196640 | tf_op jit(solution)/shard_map/ppermute | solution.py:23
  73.3 0.8 %convert_add_fusion = f32[768,128]{1,0:T(8,128)} fusion(bf16[768,128]{1,0:T(8,128)(2,1)S(1)} %collective-permute-done.11, f32[768,128]{1,0:T(8,128)S(1)} %get-tuple-element.72, bf16[768,128]{1,0:T(8,128)(2,1)S(1)} %collective-permute-done.8), kind=kLoop, calls=%fused_computation | loop fusion | flops 393216 | bytes 1179648 | tf_op jit(solution)/shard_map/add | solution.py:235
  74.1 0.0 collective-permute-done.9
  74.1 0.0 collective-permute-done.10
  74.1 0.8 %convert_add_fusion.1 = f32[768,128]{1,0:T(8,128)} fusion(bf16[768,128]{1,0:T(8,128)(2,1)S(1)} %collective-permute-done.10, f32[768,128]{1,0:T(8,128)S(1)} %get-tuple-element.65, bf16[768,128]{1,0:T(8,128)(2,1)S(1)} %collective-permute-done.9), kind=kLoop, calls=%fused_computation.1 | loop fusion | flops 393216 | bytes 1179648 | tf_op jit(solution)/shard_map/add | solution.py:234
Async XLA Ops:
  0.6 12.7 %copy-start.1 = (bf16[768,128]{1,0:T(8,128)(2,1)S(1)}, bf16[768,128]{1,0:T(8,128)(2,1)}, u32[]{:S(2)}) copy-start(bf16[768,128]{1,0:T(8,128)(2,1)} %v_ref.1) | copy-start | bytes 589828
  0.6 7.8 %copy-start = (bf16[768,128]{1,0:T(8,128)(2,1)S(1)}, bf16[768,128]{1,0:T(8,128)(2,1)}, u32[]{:S(2)}) copy-start(bf16[768,128]{1,0:T(8,128)(2,1)} %refs_0_.1) | copy-start | bytes 589828
  0.7 12.7 %copy-start.3 = (s32[256,4]{0,1:T(4,128)S(1)}, s32[256,4]{0,1:T(4,128)}, u32[]{:S(2)}) copy-start(s32[256,4]{0,1:T(4,128)} %param.15) | copy-start | bytes 12292
  0.7 12.7 %copy-start.4 = (s32[64]{0:T(128)S(1)}, s32[64]{0:T(128)}, u32[]{:S(2)}) copy-start(s32[64]{0:T(128)} %lens_ref.1) | copy-start | bytes 772
  0.7 12.7 %copy-start.2 = (f32[8,192]{1,0:T(8,128)S(1)}, f32[8,192]{1,0:T(8,128)}, u32[]{:S(2)}) copy-start(f32[8,192]{1,0:T(8,128)} %lse_ref.1) | copy-start | bytes 18436
  0.7 17.5 %collective-permute-start.2 = (bf16[768,128]{1,0:T(8,128)(2,1)}, bf16[768,128]{1,0:T(8,128)(2,1)S(1)}, u32[]{:S(2)}, u32[]{:S(2)}) collective-permute-start(bf16[768,128]{1,0:T(8,128)(2,1)} %v_ref.1), channel_id=1, source_target_pairs={{0,3},{1,4},{2,5},{3,6},{4,7},{5,8},{6,9},{7,10},{8,11},{9,12},{10... | collective-permute-start | bytes 589832 | tf_op jit(solution)/shard_map/ppermute | solution.py:23
  6.8 11.4 %collective-permute-start = (bf16[768,128]{1,0:T(8,128)(2,1)}, bf16[768,128]{1,0:T(8,128)(2,1)S(1)}, u32[]{:S(2)}, u32[]{:S(2)}) collective-permute-start(bf16[768,128]{1,0:T(8,128)(2,1)} %refs_0_.1), channel_id=1, source_target_pairs={{0,1},{1,2},{2,3},{3,4},{4,5},{5,6},{6,7},{7,8},{8,9},{9,10},{10,1... | collective-permute-start | bytes 589832 | tf_op jit(solution)/shard_map/ppermute | solution.py:23
  8.5 21.8 %collective-permute-start.4 = (bf16[768,128]{1,0:T(8,128)(2,1)S(1)}, bf16[768,128]{1,0:T(8,128)(2,1)S(1)}, u32[]{:S(2)}, u32[]{:S(2)}) collective-permute-start(bf16[768,128]{1,0:T(8,128)(2,1)S(1)} %copy-done), channel_id=1, source_target_pairs={{0,3},{1,4},{2,5},{3,6},{4,7},{5,8},{6,9},{7,10},{8,11},{9,12},{10... | collective-permute-start | bytes 589832 | tf_op jit(solution)/shard_map/ppermute | solution.py:23
  13.3 13.6 %collective-permute-start.5 = (bf16[768,128]{1,0:T(8,128)(2,1)S(1)}, bf16[768,128]{1,0:T(8,128)(2,1)S(1)}, u32[]{:S(2)}, u32[]{:S(2)}) collective-permute-start(bf16[768,128]{1,0:T(8,128)(2,1)S(1)} %copy-done.1), channel_id=1, source_target_pairs={{0,1},{1,2},{2,3},{3,4},{4,5},{5,6},{6,7},{7,8},{8,9},{9,10},{10,1... | collective-permute-start | bytes 589832 | tf_op jit(solution)/shard_map/ppermute | solution.py:23
  18.2 19.4 %collective-permute-start.1 = (bf16[768,128]{1,0:T(8,128)(2,1)S(1)}, bf16[768,128]{1,0:T(8,128)(2,1)S(1)}, u32[]{:S(2)}, u32[]{:S(2)}) collective-permute-start(bf16[768,128]{1,0:T(8,128)(2,1)S(1)} %collective-permute-done.k_ref.refs_1_), channel_id=1, source_target_pairs={{0,1},{1,2},{2,3},{3,4},{4,5},{5,6},{6,7},{7,8},{8,9},{9,10},{10,1... | collective-permute-start | bytes 589832 | tf_op jit(solution)/shard_map/ppermute | solution.py:23
  20.0 17.6 %collective-permute-start.3 = (bf16[768,128]{1,0:T(8,128)(2,1)S(1)}, bf16[768,128]{1,0:T(8,128)(2,1)S(1)}, u32[]{:S(2)}, u32[]{:S(2)}) collective-permute-start(bf16[768,128]{1,0:T(8,128)(2,1)S(1)} %collective-permute-done.2.v_ref), channel_id=1, source_target_pairs={{0,255},{1,0},{2,1},{3,2},{4,3},{5,4},{6,5},{7,6},{8,7},{9,8},{10,... | collective-permute-start | bytes 589832 | tf_op jit(solution)/shard_map/ppermute | solution.py:23
  30.2 12.8 %collective-permute-start.8 = (bf16[768,128]{1,0:T(8,128)(2,1)S(1)}, bf16[768,128]{1,0:T(8,128)(2,1)S(1)}, u32[]{:S(2)}, u32[]{:S(2)}) collective-permute-start(bf16[768,128]{1,0:T(8,128)(2,1)S(1)} %get-tuple-element.59), channel_id=1, source_target_pairs={{0,255},{1,0},{2,1},{3,2},{4,3},{5,4},{6,5},{7,6},{8,7},{9,8},{10,... | collective-permute-start | bytes 589832 | tf_op jit(solution)/shard_map/ppermute | solution.py:23
  38.4 14.1 %collective-permute-start.6 = (bf16[768,128]{1,0:T(8,128)(2,1)S(1)}, bf16[768,128]{1,0:T(8,128)(2,1)S(1)}, u32[]{:S(2)}, u32[]{:S(2)}) collective-permute-start(bf16[768,128]{1,0:T(8,128)(2,1)S(1)} %get-tuple-element.54), channel_id=1, source_target_pairs={{0,1},{1,2},{2,3},{3,4},{4,5},{5,6},{6,7},{7,8},{8,9},{9,10},{10,1... | collective-permute-start | bytes 589832 | tf_op jit(solution)/shard_map/ppermute | solution.py:23
  38.5 14.0 %collective-permute-start.7 = (bf16[768,128]{1,0:T(8,128)(2,1)S(1)}, bf16[768,128]{1,0:T(8,128)(2,1)S(1)}, u32[]{:S(2)}, u32[]{:S(2)}) collective-permute-start(bf16[768,128]{1,0:T(8,128)(2,1)S(1)} %get-tuple-element.55), channel_id=1, source_target_pairs={{0,255},{1,0},{2,1},{3,2},{4,3},{5,4},{6,5},{7,6},{8,7},{9,8},{10,... | collective-permute-start | bytes 589832 | tf_op jit(solution)/shard_map/ppermute | solution.py:23
  43.5 30.5 %collective-permute-start.9 = (bf16[768,128]{1,0:T(8,128)(2,1)S(1)}, bf16[768,128]{1,0:T(8,128)(2,1)S(1)}, u32[]{:S(2)}, u32[]{:S(2)}) collective-permute-start(bf16[768,128]{1,0:T(8,128)(2,1)S(1)} %get-tuple-element.66), channel_id=1, source_target_pairs={{0,253},{1,254},{2,255},{3,0},{4,1},{5,2},{6,3},{7,4},{8,5},{9,6},... | collective-permute-start | bytes 589832 | tf_op jit(solution)/shard_map/ppermute | solution.py:23
  52.5 20.7 %collective-permute-start.11 = (bf16[768,128]{1,0:T(8,128)(2,1)S(1)}, bf16[768,128]{1,0:T(8,128)(2,1)S(1)}, u32[]{:S(2)}, u32[]{:S(2)}) collective-permute-start(bf16[768,128]{1,0:T(8,128)(2,1)S(1)} %add_convert_fusion.1), channel_id=1, source_target_pairs={{0,253},{1,254},{2,255},{3,0},{4,1},{5,2},{6,3},{7,4},{8,5},{9,6},... | collective-permute-start | bytes 589832 | tf_op jit(solution)/shard_map/ppermute | solution.py:23
  55.1 19.0 %collective-permute-start.10 = (bf16[768,128]{1,0:T(8,128)(2,1)S(1)}, bf16[768,128]{1,0:T(8,128)(2,1)S(1)}, u32[]{:S(2)}, u32[]{:S(2)}) collective-permute-start(bf16[768,128]{1,0:T(8,128)(2,1)S(1)} %add_convert_fusion), channel_id=1, source_target_pairs={{0,255},{1,0},{2,1},{3,2},{4,3},{5,4},{6,5},{7,6},{8,7},{9,8},{10,... | collective-permute-start | bytes 589832 | tf_op jit(solution)/shard_map/ppermute | solution.py:23
